TPU v7x, 512 devices: a whole 4x8x8 slice. The times are simulated.
512 devices in a mesh: band: 8 (over x, z_hi), space: 64 (over z_lo, y, core).
Axes of the slice: x: 4, y: 8, z: 8 (z_hi: 2, z_lo: 4; z = z_hi * 4 + z_lo), core: 2. Of those that a mesh axis runs over, the one named last changes fastest.
Arguments:
- prior_orbitals: float32 [384, 64, 8, 8, 128], P('band', 'space'), may hold values from -6 to 6
- orbital_block: float32 [128, 64, 8, 8, 128], P('band', 'space'), may hold values from -6 to 6
- potential: float32 [64, 8, 8, 128], P('space'), may hold values from -2 to 1
- prior_rotation: float32 [384, 128], P('band'), may hold values from -0.25 to 0.25
- block_rotation: float32 [128, 128], replicated, may hold values from -0.25 to 0.25
Outputs:
- filtered: float32 [128, 64, 8, 8, 128], P('band', 'space')
- ritz_columns: float32 [128, 64, 8, 8, 128], P('band', 'space')
All inputs are finite; a program needn't handle non-finite values.
Results may differ from a plain program's by a relative error of at most 0.00007.
Values sent between devices are 32-bit elements; how exact they have to be, the bound alone decides.
A program may use at most 64 MiB of HBM per device.

v0:
```python
import jax
import jax.numpy as jnp
from jax import lax
from jax.sharding import PartitionSpec as P

stencil_taps = (
    -5369.0 / 1800.0,
    12.0 / 7.0,
    -15.0 / 56.0,
    10.0 / 189.0,
    -1.0 / 112.0,
    2.0 / 1925.0,
    -1.0 / 16632.0,
)
stencil_reach = 6
shift_center = 6.0
half_range = 5.0


def padded_2(cells, sides, width):
    for axis, dim in sides:
        count = lax.axis_size(axis)
        ends = count - 1
        head = lax.slice_in_dim(cells, 0, width, axis=dim)
        tail = lax.slice_in_dim(cells, cells.shape[dim] - width, cells.shape[dim], axis=dim)
        cells = jnp.concatenate(
            [
                lax.ppermute(tail, axis, [(i, (i + 1) % count) for i in range(ends)]),
                cells,
                lax.ppermute(head, axis, [((i + 1) % count, i) for i in range(ends)]),
            ],
            axis=dim,
        )
    return cells


def second_along(padded, axis_number, length):
    summed = stencil_taps[0] * lax.slice_in_dim(
        padded, stencil_reach, stencil_reach + length, axis=axis_number
    )
    for offset in range(1, stencil_reach + 1):
        ahead = lax.slice_in_dim(
            padded, stencil_reach + offset, stencil_reach + offset + length, axis=axis_number
        )
        behind = lax.slice_in_dim(
            padded, stencil_reach - offset, stencil_reach - offset + length, axis=axis_number
        )
        summed = summed + stencil_taps[offset] * (ahead + behind)
    return summed


def hamiltonian(values_in, potential_here):
    cells_x = values_in.shape[1]
    cells_y = values_in.shape[2]
    cells_z = values_in.shape[3]
    pad_y = padded_2(values_in, (("space", 2),), stencil_reach)
    pad_x = jnp.pad(values_in, ((0, 0), (stencil_reach, stencil_reach), (0, 0), (0, 0)))
    pad_z = jnp.pad(values_in, ((0, 0), (0, 0), (0, 0), (stencil_reach, stencil_reach)))
    laplace = (
        second_along(pad_x, 1, cells_x)
        + second_along(pad_y, 2, cells_y)
        + second_along(pad_z, 3, cells_z)
    )
    return -0.5 * laplace + potential_here * values_in


def rotate(weights, orbitals):
    return jnp.einsum(
        "on,oxyz->nxyz",
        weights,
        orbitals,
        precision=lax.Precision.HIGHEST,
        preferred_element_type=jnp.float32,
    )


def shards(prior_orbitals, orbital_block, potential, prior_rotation, block_rotation):
    prior_here = prior_orbitals[:, 0]
    start_here = orbital_block[:, 0]
    potential_here = potential[0]
    own_block = start_here.shape[0]
    band_index = lax.axis_index("band")
    first_step = (hamiltonian(start_here, potential_here) - shift_center * start_here) / half_range
    second_step = (
        2.0 * (hamiltonian(first_step, potential_here) - shift_center * first_step) / half_range
        - start_here
    )
    block_rows = lax.dynamic_slice_in_dim(block_rotation, band_index * own_block, own_block, 0)
    ritz_here = lax.psum_scatter(
        (rotate(prior_rotation, prior_here) + rotate(block_rows, second_step))[:, None],
        "band",
        scatter_dimension=0,
        tiled=True,
    )
    return (second_step[:, None], ritz_here)


def solution(mesh):
    placed = (
        P("band", "space", None, None, None),
        P("band", "space", None, None, None),
        P("space", None, None, None),
        P("band", None),
        P(),
    )
    return jax.shard_map(
        shards,
        mesh=mesh,
        in_specs=placed,
        out_specs=(P("band", "space", None, None, None), P("band", "space", None, None, None)),
        check_vma=False,
    )
```

profile of v0, /device:TPU:56, one launch (start us, length us, event | category | flops | bytes accessed | tf_op | source)
XLA Modules:
  0.0 201.6 jit_solution(7329409996726597944)
XLA Ops:
  7.2 0.0 copy-start
  7.2 0.0 copy-start.1
  7.2 0.0 copy-start.3
  7.2 0.0 reduce-scatter.2.cloned.1.call-start
  7.2 1.4 fusion.149
  8.7 2.7 %collective-permute-start = (f32[16,8,6,128]{3,2,1,0:T(8,128)S(1)}, f32[16,8,6,128]{3,2,1,0:T(8,128)S(1)}, u32[]{:S(2)}, u32[]{:S(2)}) collective-permute-start(f32[16,8,6,128]{3,2,1,0:T(8,128)S(1)} %get-tuple-element.8), channel_id=1, source_target_pairs={{1,0},{2,1},{3,2},{4,3},{5,4},{6,5},{7,6},{8,7},{9,8},{10,9},{11,1... | collective-permute-start | bytes 1179656 | tf_op jit(solution)/shard_map/ppermute | solution.py:30
  11.4 1.9 collective-permute-start.1
  13.3 4.7 %collective-permute-done = f32[16,8,6,128]{3,2,1,0:T(8,128)S(1)} collective-permute-done((f32[16,8,6,128]{3,2,1,0:T(8,128)S(1)}, f32[16,8,6,128]{3,2,1,0:T(8,128)S(1)}, u32[]{:S(2)}, u32[]{:S(2)}) %collective-permute-start) | collective-permute-done | bytes 393248 | tf_op jit(solution)/shard_map/ppermute | solution.py:30
  18.1 3.8 %collective-permute-done.1 = f32[16,8,6,128]{3,2,1,0:T(8,128)S(1)} collective-permute-done((f32[16,8,6,128]{3,2,1,0:T(8,128)S(1)}, f32[16,8,6,128]{3,2,1,0:T(8,128)S(1)}, u32[]{:S(2)}, u32[]{:S(2)}) %collective-permute-start.1) | collective-permute-done | bytes 393248 | tf_op jit(solution)/shard_map/ppermute | solution.py:28
  21.9 0.0 copy-done.1
  21.9 2.3 %broadcast_multiply_fusion = (f32[16,8,8,128]{3,2,1,0:T(8,128)S(1)}, f32[16,8,8,128]{3,2,1,0:T(8,128)S(1)}) fusion(f32[16,8,8,128]{3,2,1,0:T(8,128)S(1)} %bitcast.20, f32[8,8,128]{2,1,0:T(8,128)S(1)} %bitcast.22, f32[16,8,6,128]{3,2,1,0:T(8,128)S(1)} %collective-permute-done.1, f32[16,8,6,128]{3,2,1,0:T(8,128)S(1)} %collective-permute-done), kind=kLoop, calls=%fused_computation.236 | loop fusion | flops 9830400 | bytes 2392064 | tf_op jit(solution)/shard_map/div | solution.py:83
  24.2 1.1 fusion.148
  25.3 1.9 collective-permute-start.2
  27.2 2.4 %collective-permute-start.3 = (f32[16,8,6,128]{3,2,1,0:T(8,128)}, f32[16,8,6,128]{3,2,1,0:T(8,128)}, u32[]{:S(2)}, u32[]{:S(2)}) collective-permute-start(f32[16,8,6,128]{3,2,1,0:T(8,128)} %get-tuple-element.7), channel_id=1, source_target_pairs={{0,1},{1,2},{2,3},{3,4},{4,5},{5,6},{6,7},{7,8},{8,9},{9,10},{10,1... | collective-permute-start | bytes 1179656 | tf_op jit(solution)/shard_map/ppermute | solution.py:28
  29.7 4.6 %collective-permute-done.2 = f32[16,8,6,128]{3,2,1,0:T(8,128)} collective-permute-done((f32[16,8,6,128]{3,2,1,0:T(8,128)}, f32[16,8,6,128]{3,2,1,0:T(8,128)}, u32[]{:S(2)}, u32[]{:S(2)}) %collective-permute-start.2) | collective-permute-done | bytes 393248 | tf_op jit(solution)/shard_map/ppermute | solution.py:30
  34.2 3.8 %collective-permute-done.3 = f32[16,8,6,128]{3,2,1,0:T(8,128)} collective-permute-done((f32[16,8,6,128]{3,2,1,0:T(8,128)}, f32[16,8,6,128]{3,2,1,0:T(8,128)}, u32[]{:S(2)}, u32[]{:S(2)}) %collective-permute-start.3) | collective-permute-done | bytes 393248 | tf_op jit(solution)/shard_map/ppermute | solution.py:28
  38.1 5.6 %fusion.12 = f32[16,8,8,128]{3,2,1,0:T(8,128)S(1)} fusion(f32[16,8,6,128]{3,2,1,0:T(8,128)} %collective-permute-done.3, f32[16,8,8,128]{3,2,1,0:T(8,128)S(1)} %get-tuple-element.4, f32[16,8,6,128]{3,2,1,0:T(8,128)} %collective-permute-done.2, f32[16,8,8,128]{3,2,1,0:T(8,128)S(1)} %get-tuple-element.5, f32[8,8,128]{2,1,0:T(8,128)S(1)} %broadcast_multiply_fusion.1, ...), kind=kLoop, calls=%fused_computation.101 | loop fusion | flops 9961472 | bytes 2916352 | tf_op jit(solution)/shard_map/sub | solution.py:85
  43.7 0.0 copy-start.2
  43.7 0.0 copy-start.4
  43.7 4.3 %fusion.141 = f32[128,8,8,128]{3,0,2,1:T(8,128)S(1)} fusion(f32[16,8,8,128]{3,2,1,0:T(8,128)S(1)} %fusion.12, f32[128,128]{1,0:T(8,128)} %param.9, s32[]{:T(128)S(6)} %select_n.3), kind=kOutput, calls=%fused_computation.234 | convolution fusion | flops 201326592 | bytes 4726788 | tf_op jit(solution)/shard_map/on,oxyz->nxyz/dot_general | solution.py:68
  48.0 5.5 %add_bitcast_fusion = f32[128,1,8,8,128]{4,0,3,2,1:T(8,128)} fusion(f32[128,8,8,128]{3,0,2,1:T(8,128)S(1)} %fusion.141, f32[48,8,8,128]{3,2,1,0:T(8,128)S(1)} %bitcast.18, f32[48,128]{1,0:T(8,128)S(1)} %copy-done.4), kind=kOutput, calls=%fused_computation.24 | convolution fusion | flops 605028352 | bytes 9986048 | tf_op jit(solution)/shard_map/on,oxyz->nxyz/dot_general | solution.py:68
  53.6 0.0 reduce-scatter.2.cloned.1.call-update
  53.6 139.1 %reduce-scatter.2.cloned.1.call-done = f32[16,1,8,8,128]{4,0,3,2,1:T(8,128)} async-done(((f32[128,1,8,8,128]{4,0,3,2,1:T(8,128)}), f32[16,1,8,8,128]{4,0,3,2,1:T(8,128)}) %reduce-scatter.2.cloned.1.call-update) | async-done | bytes 524304 | tf_op jit(solution)/shard_map/reduce_scatter | solution.py:89
  192.7 2.0 copy.9
  (5 shorter events, 0.0 us)
Async XLA Ops:
  7.2 40.8 %copy-start = (f32[48,1,8,8,128]{4,3,2,1,0:T(8,128)S(1)}, f32[48,1,8,8,128]{4,3,2,1,0:T(8,128)}, u32[]{:S(2)}) copy-start(f32[48,1,8,8,128]{4,3,2,1,0:T(8,128)} %param.5) | copy-start | bytes 4718596
  7.2 14.7 %copy-start.1 = (f32[16,1,8,8,128]{4,3,2,1,0:T(8,128)S(1)}, f32[16,1,8,8,128]{4,3,2,1,0:T(8,128)}, u32[]{:S(2)}) copy-start(f32[16,1,8,8,128]{4,3,2,1,0:T(8,128)} %param.6) | copy-start | bytes 1572868
  7.2 14.7 %copy-start.3 = (f32[1,8,8,128]{3,2,1,0:T(8,128)S(1)}, f32[1,8,8,128]{3,2,1,0:T(8,128)}, u32[]{:S(2)}) copy-start(f32[1,8,8,128]{3,2,1,0:T(8,128)} %param.7) | copy-start | bytes 98308
  7.2 185.5 %reduce-scatter.2.cloned.1.call-start = ((), (), s32[]{:S(2)}) async-start(), calls=%async_computation.1 | async-start | bytes 4718592 | tf_op jit(solution)/shard_map/reduce_scatter | solution.py:89
  8.7 9.4 %collective-permute-start = (f32[16,8,6,128]{3,2,1,0:T(8,128)S(1)}, f32[16,8,6,128]{3,2,1,0:T(8,128)S(1)}, u32[]{:S(2)}, u32[]{:S(2)}) collective-permute-start(f32[16,8,6,128]{3,2,1,0:T(8,128)S(1)} %get-tuple-element.8), channel_id=1, source_target_pairs={{1,0},{2,1},{3,2},{4,3},{5,4},{6,5},{7,6},{8,7},{9,8},{10,9},{11,1... | collective-permute-start | bytes 1179656 | tf_op jit(solution)/shard_map/ppermute | solution.py:30
  11.4 10.5 %collective-permute-start.1 = (f32[16,8,6,128]{3,2,1,0:T(8,128)S(1)}, f32[16,8,6,128]{3,2,1,0:T(8,128)S(1)}, u32[]{:S(2)}, u32[]{:S(2)}) collective-permute-start(f32[16,8,6,128]{3,2,1,0:T(8,128)S(1)} %get-tuple-element.9), channel_id=1, source_target_pairs={{0,1},{1,2},{2,3},{3,4},{4,5},{5,6},{6,7},{7,8},{8,9},{9,10},{10,1... | collective-permute-start | bytes 1179656 | tf_op jit(solution)/shard_map/ppermute | solution.py:28
  25.3 8.9 %collective-permute-start.2 = (f32[16,8,6,128]{3,2,1,0:T(8,128)}, f32[16,8,6,128]{3,2,1,0:T(8,128)}, u32[]{:S(2)}, u32[]{:S(2)}) collective-permute-start(f32[16,8,6,128]{3,2,1,0:T(8,128)} %get-tuple-element.6), channel_id=1, source_target_pairs={{1,0},{2,1},{3,2},{4,3},{5,4},{6,5},{7,6},{8,7},{9,8},{10,9},{11,1... | collective-permute-start | bytes 1179656 | tf_op jit(solution)/shard_map/ppermute | solution.py:30
  27.2 10.8 %collective-permute-start.3 = (f32[16,8,6,128]{3,2,1,0:T(8,128)}, f32[16,8,6,128]{3,2,1,0:T(8,128)}, u32[]{:S(2)}, u32[]{:S(2)}) collective-permute-start(f32[16,8,6,128]{3,2,1,0:T(8,128)} %get-tuple-element.7), channel_id=1, source_target_pairs={{0,1},{1,2},{2,3},{3,4},{4,5},{5,6},{6,7},{7,8},{8,9},{9,10},{10,1... | collective-permute-start | bytes 1179656 | tf_op jit(solution)/shard_map/ppermute | solution.py:28
  43.7 4.3 %copy-start.2 = (f32[16,8,8,128]{3,2,1,0:T(8,128)}, f32[16,8,8,128]{3,2,1,0:T(8,128)S(1)}, u32[]{:S(2)}) copy-start(f32[16,8,8,128]{3,2,1,0:T(8,128)S(1)} %fusion.12) | copy-start | bytes 1572868
  43.7 4.3 %copy-start.4 = (f32[48,128]{1,0:T(8,128)S(1)}, f32[48,128]{1,0:T(8,128)}, u32[]{:S(2)}) copy-start(f32[48,128]{1,0:T(8,128)} %param.8) | copy-start | bytes 73732
Sparse Core Ops, SparseCore 0:
  53.7 138.9 reduce-scatter.1
where the time goes:
time: 202 us
  waiting for transfers between devices  156 us (77%)
  between operations  14.2 us (7%)
  matrix products  9.79 us (5%)
  starting transfers between devices  8.97 us (4%)
  other arithmetic  7.97 us (4%)
  local copies, waits for them, and re-layouts  4.55 us (2%)
    reduce_scatter x1, waiting for transfers between devices, shards(): lax.psum_scatter((rotate(prior_rotation, prior_here) + rotate(block_rows,...  139 us
    dot_general x2, matrix products, rotate(): jnp.einsum('on,oxyz->nxyz', weights, orbitals, precision=lax.Precision.HI...  9.79 us
    ppermute x2, waiting for transfers between devices, padded_2(): lax.ppermute(head, axis, [((i + 1) % count, i) for i in range(ends)])  9.31 us
    ppermute x2, waiting for transfers between devices, padded_2(): lax.ppermute(tail, axis, [(i, (i + 1) % count) for i in range(ends)])  7.65 us
    sub x1, other arithmetic, shards(): 2.0 * (hamiltonian(first_step, potential_here) - shift_center * first_step)  5.64 us
    ppermute x2, starting transfers between devices, padded_2(): lax.ppermute(head, axis, [((i + 1) % count, i) for i in range(ends)])  4.61 us
    ppermute x2, starting transfers between devices, padded_2(): lax.ppermute(tail, axis, [(i, (i + 1) % count) for i in range(ends)])  4.33 us
  transfers between devices with their start and end apart: 5, of which 5 were waited for; matrix products, arithmetic and copies ran while one was open for 0% of the time, Pallas kernels for 0%

commit v1 on v0

v1 whole, which is shorter than its diff:
```python
import functools

import jax
import jax.numpy as jnp
from jax import lax
from jax.experimental import pallas as pl
from jax.experimental.pallas import tpu as pltpu
from jax.sharding import PartitionSpec as P

stencil_taps = (
    -5369.0 / 1800.0,
    12.0 / 7.0,
    -15.0 / 56.0,
    10.0 / 189.0,
    -1.0 / 112.0,
    2.0 / 1925.0,
    -1.0 / 16632.0,
)
reach = 6
shift_center = 6.0
half_range = 5.0
lap_scale = -0.5 / half_range

NB = 16
NP = 48
CX = 8
CY = 8
CZ = 128
XS = 4
ZH = 2
NCOL = 128
CHUNKS = 4
PER = NB // CHUNKS
MESH = pl.DeviceIdType.MESH
f32 = jnp.float32
bf16 = jnp.bfloat16


def split(values):
    high = values.astype(bf16)
    low = (values - high.astype(f32)).astype(bf16)
    return high, low


def dot(lhs, rhs):
    return jnp.dot(lhs, rhs, preferred_element_type=f32)


def stencil(ext, at, band, diagonal):
    cells = ext[at, :, 8:16, :]
    high, low = split(cells.reshape(CX * CY, CZ))
    along_z = dot(jnp.concatenate([high, low, high], axis=1), band[...]).reshape(CX, CY, CZ)
    planes = [cells[i] for i in range(CX)]
    rows = []
    for i in range(CX):
        total = along_z[i] + diagonal[i] * planes[i]
        for k in range(1, reach + 1):
            near = ext[at, i, 8 - k : 16 - k, :] + ext[at, i, 8 + k : 16 + k, :]
            if i - k >= 0:
                near = near + planes[i - k]
            if i + k < CX:
                near = near + planes[i + k]
            total = total + (lap_scale * stencil_taps[k]) * near
        rows.append(total)
    return rows


def kernel(
    slabs,
    prior,
    block,
    pot,
    prior_rot,
    block_rot,
    filtered_out,
    ritz_out,
    ext0,
    ext1,
    fil,
    gp,
    gf,
    wp,
    wp_high,
    wp_low,
    wf,
    band,
    diagonal,
    pp,
    zr,
    sm,
    local_sem,
    halo_send,
    halo_recv,
    wp_send,
    wp_recv,
    gp_send,
    gp_recv,
    gf_send,
    gf_recv,
    z_send,
    z_recv,
    out_send,
    out_recv,
):
    b = lax.axis_index("band")
    d = lax.axis_index("space")
    x = lax.div(b, ZH)
    zh = lax.rem(b, ZH)
    has_prev = d > 0
    has_next = d < slabs - 1

    def x_of(r):
        return lax.rem(x + r, XS)

    def x_peer(r):
        return (x_of(r) * ZH + zh, d)

    z_peer = (x * ZH + (1 - zh), d)
    prev_peer = (b, jnp.maximum(d - 1, 0))
    next_peer = (b, jnp.minimum(d + 1, slabs - 1))

    barrier = pltpu.get_barrier_semaphore()
    for r in range(1, XS):
        pl.semaphore_signal(barrier, inc=1, device_id=x_peer(r), device_id_type=MESH)
    pl.semaphore_signal(barrier, inc=1, device_id=z_peer, device_id_type=MESH)

    @pl.when(has_prev)
    def _():
        pl.semaphore_signal(barrier, inc=1, device_id=prev_peer, device_id_type=MESH)

    @pl.when(has_next)
    def _():
        pl.semaphore_signal(barrier, inc=1, device_id=next_peer, device_id_type=MESH)

    def remote(src, dst, send, recv, peer):
        return pltpu.make_async_remote_copy(
            src_ref=src, dst_ref=dst, send_sem=send, recv_sem=recv, device_id=peer, device_id_type=MESH
        )

    def chunk(c):
        return pl.ds(c * PER, PER)

    own_block = [
        pltpu.make_async_copy(block.at[chunk(c), 0], ext0.at[chunk(c), :, pl.ds(8, 8), :], local_sem.at[c])
        for c in range(CHUNKS)
    ]
    own_prior = [
        pltpu.make_async_copy(prior.at[:, 0, 2 * x + xp], gp.at[xp, x], local_sem.at[CHUNKS + xp])
        for xp in range(2)
    ]
    own_fil = [
        pltpu.make_async_copy(
            fil.at[chunk(c), pl.ds(2 * x, 2)], gf.at[x, chunk(c)], local_sem.at[CHUNKS + 2 + c]
        )
        for c in range(CHUNKS)
    ]
    out_fil = [
        pltpu.make_async_copy(
            fil.at[chunk(c)], filtered_out.at[chunk(c), 0], local_sem.at[2 * CHUNKS + 2 + c]
        )
        for c in range(CHUNKS)
    ]
    own_ritz = [
        pltpu.make_async_copy(
            sm.at[xp, x], ritz_out.at[:, 0, 2 * x + xp], local_sem.at[3 * CHUNKS + 2 + xp]
        )
        for xp in range(2)
    ]

    up0 = [
        remote(
            block.at[chunk(c), 0, :, pl.ds(2, 6), :],
            ext0.at[chunk(c), :, pl.ds(2, 6), :],
            halo_send.at[0, c],
            halo_recv.at[0, c],
            next_peer,
        )
        for c in range(CHUNKS)
    ]
    down0 = [
        remote(
            block.at[chunk(c), 0, :, pl.ds(0, 6), :],
            ext0.at[chunk(c), :, pl.ds(16, 6), :],
            halo_send.at[1, c],
            halo_recv.at[1, c],
            prev_peer,
        )
        for c in range(CHUNKS)
    ]
    up1 = [
        remote(
            ext1.at[chunk(c), :, pl.ds(10, 6), :],
            ext1.at[chunk(c), :, pl.ds(2, 6), :],
            halo_send.at[2, c],
            halo_recv.at[2, c],
            next_peer,
        )
        for c in range(CHUNKS)
    ]
    down1 = [
        remote(
            ext1.at[chunk(c), :, pl.ds(8, 6), :],
            ext1.at[chunk(c), :, pl.ds(16, 6), :],
            halo_send.at[3, c],
            halo_recv.at[3, c],
            prev_peer,
        )
        for c in range(CHUNKS)
    ]

    weights_x = [
        remote(prior_rot, wp.at[x], wp_send.at[r - 1], wp_recv.at[r - 1], x_peer(r)) for r in range(1, XS)
    ]
    prior_x = [
        [
            remote(
                prior.at[:, 0, 2 * x_of(r) + xp],
                gp.at[xp, x],
                gp_send.at[xp, r - 1],
                gp_recv.at[xp, r - 1],
                x_peer(r),
            )
            for r in range(1, XS)
        ]
        for xp in range(2)
    ]
    fil_x = [
        [
            remote(
                fil.at[chunk(c), pl.ds(2 * x_of(r), 2)],
                gf.at[x, chunk(c)],
                gf_send.at[c, r - 1],
                gf_recv.at[c, r - 1],
                x_peer(r),
            )
            for r in range(1, XS)
        ]
        for c in range(CHUNKS)
    ]

    def z_copy(xp, xd):
        rows = pl.ds((xd * ZH + (1 - zh)) * NB, NB)
        return remote(pp.at[xp, rows], zr.at[xp, xd], z_send.at[xp, xd], z_recv.at[xp, xd], z_peer)

    def out_copy(xp, r):
        return remote(
            sm.at[xp, x_of(r)],
            ritz_out.at[:, 0, 2 * x + xp],
            out_send.at[xp, r - 1],
            out_recv.at[xp, r - 1],
            x_peer(r),
        )

    for copy in own_block + own_prior:
        copy.start()

    row = lax.broadcasted_iota(jnp.int32, (CZ, CZ), 0)
    col = lax.broadcasted_iota(jnp.int32, (CZ, CZ), 1)
    apart = jnp.abs(row - col)
    taps = jnp.zeros((CZ, CZ), f32)
    for k in range(1, reach + 1):
        taps = jnp.where(apart == k, lap_scale * stencil_taps[k], taps)
    taps_high, taps_low = split(taps)
    band[0:CZ, :] = taps_high
    band[CZ : 2 * CZ, :] = taps_high
    band[2 * CZ : 3 * CZ, :] = taps_low
    diagonal[...] = pot[0] * (1.0 / half_range) + (
        3.0 * lap_scale * stencil_taps[0] - shift_center / half_range
    )

    @pl.when(jnp.logical_not(has_prev))
    def _():
        ext0[:, :, 0:8, :] = jnp.zeros((NB, CX, 8, CZ), f32)
        ext1[:, :, 0:8, :] = jnp.zeros((NB, CX, 8, CZ), f32)

    @pl.when(jnp.logical_not(has_next))
    def _():
        ext0[:, :, 16:24, :] = jnp.zeros((NB, CX, 8, CZ), f32)
        ext1[:, :, 16:24, :] = jnp.zeros((NB, CX, 8, CZ), f32)

    pl.semaphore_wait(
        barrier, XS + jnp.where(has_prev, 1, 0) + jnp.where(has_next, 1, 0)
    )

    def start_halo(up, down):
        @pl.when(has_next)
        def _():
            up.start()

        @pl.when(has_prev)
        def _():
            down.start()

    def wait_halo(up, down):
        @pl.when(has_prev)
        def _():
            up.wait_recv()

        @pl.when(has_next)
        def _():
            down.wait_recv()

    for c in range(CHUNKS):
        start_halo(up0[c], down0[c])
    for copy in weights_x + prior_x[0]:
        copy.start()

    for c in range(CHUNKS):
        own_block[c].wait()
        wait_halo(up0[c], down0[c])

        def first(j, carry):
            at = c * PER + j
            rows = stencil(ext0, at, band, diagonal)
            for i in range(CX):
                ext1[at, i, 8:16, :] = rows[i]
            return carry

        lax.fori_loop(0, PER, first, 0)
        start_halo(up1[c], down1[c])

    for c in range(CHUNKS):
        wait_halo(up1[c], down1[c])

        def second(j, carry):
            at = c * PER + j
            rows = stencil(ext1, at, band, diagonal)
            for i in range(CX):
                fil[at, i] = 2.0 * rows[i] - ext0[at, i, 8:16, :]
            return carry

        lax.fori_loop(0, PER, second, 0)
        for copy in fil_x[c] + [own_fil[c], out_fil[c]]:
            copy.start()
    for copy in prior_x[1]:
        copy.start()

    wp[x] = prior_rot[...]
    for copy in weights_x:
        copy.wait_recv()
    turned = jnp.concatenate([wp[s] for s in range(XS)], axis=0).T
    wp_high[...], wp_low[...] = split(turned)
    own_rows = jnp.concatenate(
        [block_rot[pl.ds(pl.multiple_of((s * ZH + zh) * NB, NB), NB), :] for s in range(XS)], axis=0
    )
    rows_high, rows_low = split(own_rows)
    stacked = jnp.concatenate([rows_high, rows_high, rows_low], axis=0).astype(f32)
    wf[...] = stacked.T.astype(bf16)

    gf_rows = gf.reshape(XS * NB * 2 * CY, CZ)

    def prior_part(xp):
        own_prior[xp].wait()
        for copy in prior_x[xp]:
            copy.wait_recv()
        gp_rows = gp.at[xp].reshape(XS * NP * CY, CZ)
        pp_rows = pp.at[xp].reshape(NCOL * CY, CZ)
        for y in range(0, CY, 2):
            values = jnp.concatenate(
                [gp_rows[pl.ds(y + h, XS * NP, stride=CY), :] for h in range(2)], axis=1
            )
            high, low = split(values)
            total = dot(wp_high[...], high) + dot(wp_high[...], low) + dot(wp_low[...], high)
            for h in range(2):
                pp_rows[pl.ds(y + h, NCOL, stride=CY), :] = total[:, h * CZ : (h + 1) * CZ]

    def block_part(xp):
        pp_rows = pp.at[xp].reshape(NCOL * CY, CZ)
        for y in range(0, CY, 2):
            values = jnp.concatenate(
                [gf_rows[pl.ds(xp * CY + y + h, XS * NB, stride=2 * CY), :] for h in range(2)], axis=1
            )
            high, low = split(values)
            total = dot(wf[...], jnp.concatenate([high, low, high], axis=0))
            for h in range(2):
                at = pl.ds(y + h, NCOL, stride=CY)
                pp_rows[at, :] = pp_rows[at, :] + total[:, h * CZ : (h + 1) * CZ]
        for xd in range(XS):
            z_copy(xp, xd).start()

    prior_part(0)
    for c in range(CHUNKS):
        own_fil[c].wait()
        for copy in fil_x[c]:
            copy.wait_recv()
    block_part(0)
    prior_part(1)
    block_part(1)

    for xp in range(2):
        for xd in range(XS):
            z_copy(xp, xd).wait_recv()
            sm[xp, xd] = pp[xp, pl.ds((xd * ZH + zh) * NB, NB)] + zr[xp, xd]
        for r in range(1, XS):
            out_copy(xp, r).start()
        own_ritz[xp].start()

    for xp in range(2):
        own_ritz[xp].wait()
        for r in range(1, XS):
            out_copy(xp, r).wait()
        for xd in range(XS):
            z_copy(xp, xd).wait_send()
        for copy in prior_x[xp]:
            copy.wait_send()
    for copy in weights_x:
        copy.wait_send()
    for c in range(CHUNKS):
        out_fil[c].wait()
        for copy in fil_x[c]:
            copy.wait_send()

        @pl.when(has_next)
        def _():
            up0[c].wait_send()
            up1[c].wait_send()

        @pl.when(has_prev)
        def _():
            down0[c].wait_send()
            down1[c].wait_send()


def shards(prior_orbitals, orbital_block, potential, prior_rotation, block_rotation):
    slabs = lax.axis_size("space")
    whole = pl.BlockSpec(memory_space=pltpu.VMEM)
    anywhere = pl.BlockSpec(memory_space=pl.ANY)
    dma = pltpu.SemaphoreType.DMA
    return pl.pallas_call(
        functools.partial(kernel, slabs),
        out_shape=(
            jax.ShapeDtypeStruct((NB, 1, CX, CY, CZ), f32),
            jax.ShapeDtypeStruct((NB, 1, CX, CY, CZ), f32),
        ),
        in_specs=[anywhere, anywhere, whole, whole, whole],
        out_specs=(anywhere, anywhere),
        scratch_shapes=[
            pltpu.VMEM((NB, CX, 24, CZ), f32),
            pltpu.VMEM((NB, CX, 24, CZ), f32),
            pltpu.VMEM((NB, CX, CY, CZ), f32),
            pltpu.VMEM((2, XS, NP, CY, CZ), f32),
            pltpu.VMEM((XS, NB, 2, CY, CZ), f32),
            pltpu.VMEM((XS, NP, NCOL), f32),
            pltpu.VMEM((NCOL, XS * NP), bf16),
            pltpu.VMEM((NCOL, XS * NP), bf16),
            pltpu.VMEM((NCOL, 3 * XS * NB), bf16),
            pltpu.VMEM((3 * CZ, CZ), bf16),
            pltpu.VMEM((CX, CY, CZ), f32),
            pltpu.VMEM((2, NCOL, CY, CZ), f32),
            pltpu.VMEM((2, XS, NB, CY, CZ), f32),
            pltpu.VMEM((2, XS, NB, CY, CZ), f32),
            dma((3 * CHUNKS + 4,)),
            dma((4, CHUNKS)),
            dma((4, CHUNKS)),
            dma((XS - 1,)),
            dma((XS - 1,)),
            dma((2, XS - 1)),
            dma((2, XS - 1)),
            dma((CHUNKS, XS - 1)),
            dma((CHUNKS, XS - 1)),
            dma((2, XS)),
            dma((2, XS)),
            dma((2, XS - 1)),
            dma((2, XS - 1)),
        ],
        compiler_params=pltpu.CompilerParams(
            collective_id=0, has_side_effects=True, vmem_limit_bytes=56 * 1024 * 1024
        ),
        cost_estimate=pl.CostEstimate(
            flops=3 * 2 * 256 * 128 * 2048, bytes_accessed=4 * 1024 * 1024, transcendentals=0
        ),
        name="filter_and_rotate",
    )(prior_orbitals, orbital_block, potential, prior_rotation, block_rotation)


def solution(mesh):
    placed = (
        P("band", "space", None, None, None),
        P("band", "space", None, None, None),
        P("space", None, None, None),
        P("band", None),
        P(),
    )
    return jax.shard_map(
        shards,
        mesh=mesh,
        in_specs=placed,
        out_specs=(P("band", "space", None, None, None), P("band", "space", None, None, None)),
        check_vma=False,
    )
```

time: 202 us -> 69 us (0.34)
  waiting for transfers between devices: 156 us -> 0 us
  Pallas kernels: 0 us -> 64.3 us
  between operations: 14.2 us -> 0.64 us
  matrix products: 9.79 us -> 0 us
  starting transfers between devices: 8.97 us -> 0 us
  other arithmetic: 7.97 us -> 0 us
    reduce_scatter x1 -> x0, waiting for transfers between devices: 139 us -> none  [shards(): lax.psum_scatter((rotate(prior_rotation, prior_here) + rotate(block_rows,...]
    pallas_call x0 -> x1, Pallas kernels: none -> 64.3 us  [shards(): pl.pallas_call(functools.partial(kernel, slabs), out_shape=(jax.ShapeDtyp...]
    ppermute x4 -> x0, waiting for transfers between devices: 17 us -> none  [the longest x2 9.31 us: padded_2(): lax.ppermute(head, axis, [((i + 1) % count, i) for i in range(ends)])]
    dot_general x2 -> x0, matrix products: 9.79 us -> none  [rotate(): jnp.einsum('on,oxyz->nxyz', weights, orbitals, precision=lax.Precision.HI...]
    ppermute x4 -> x0, starting transfers between devices: 8.93 us -> none  [the longest x2 4.61 us: padded_2(): lax.ppermute(head, axis, [((i + 1) % count, i) for i in range(ends)])]
    sub x1 -> x0, other arithmetic: 5.64 us -> none  [shards(): 2.0 * (hamiltonian(first_step, potential_here) - shift_center * first_step)]
    slice x2 -> x0, local copies, waits for them, and re-layouts: 2.52 us -> none  [padded_2(): head = lax.slice_in_dim(cells, 0, width, axis=dim)]
    div x1 -> x0, other arithmetic: 2.33 us -> none  [shards(): (hamiltonian(start_here, potential_here) - shift_center * start_here) / h...]
  transfers between devices with their start and end apart: 5 -> 0, of which waited for: 5 -> 0; matrix products, arithmetic and copies ran while one was open for 0% -> 0% of each run, Pallas kernels for 0% -> 0%
where the time goes in v1:
time: 69 us; the launch traced here: 68.7 us
  Pallas kernels  64.3 us (93%)
  local copies, waits for them, and re-layouts  3.77 us (5%)
    pallas_call x1, Pallas kernels, shards(): pl.pallas_call(functools.partial(kernel, slabs), out_shape=(jax.ShapeDtyp...  64.3 us
    unnamed x2, local copies, waits for them, and re-layouts  3.77 us

profile of v1, /device:TPU:56, one launch (start us, length us, event | category | flops | bytes accessed | tf_op | source)
XLA Modules:
  0.0 68.7 jit_solution(18151904044748716116)
XLA Ops:
  0.6 64.3 %filter_and_rotate.1 = (f32[16,1,8,8,128]{4,3,2,1,0:T(8,128)}, f32[16,1,8,8,128]{4,3,2,1,0:T(8,128)}) custom-call(f32[48,1,8,8,128]{4,3,2,1,0:T(8,128)} %prior.1, f32[16,1,8,8,128]{4,3,2,1,0:T(8,128)} %block.1, f32[1,8,8,128]{3,2,1,0:T(8,128)} %pot.1, f32[48,128]{1,0:T(8,128)} %prior_rot.1, f32[128,128]{1,0:T(8,128)} %block_rot.1), custom_call_target="tpu_custom_call" | custom-call | flops 402653184 | bytes 4194304 | tf_op jit(solution)/shard_map/filter_and_rotate/pallas_call | solution.py:429
  64.9 1.9 %copy.9 = f32[16,1,8,8,128]{4,3,2,1,0:T(8,128)} copy(f32[16,1,8,8,128]{4,3,2,1,0:T(8,128)} %get-tuple-element.4) | data formatting | bytes 1048576
  66.8 1.9 %copy.10 = f32[16,1,8,8,128]{4,3,2,1,0:T(8,128)} copy(f32[16,1,8,8,128]{4,3,2,1,0:T(8,128)} %get-tuple-element.5) | data formatting | bytes 1048576

commit v2 on v1

--- a/solution.py
+++ b/solution.py
@@ -30,6 +30,10 @@
 ZH = 2
 NCOL = 128
 CHUNKS = 4
+WINDOW = 16
+LAG = 8
+HALF = CY // 2
+ORDER = (2, 1, 3, 0)
 PER = NB // CHUNKS
 MESH = pl.DeviceIdType.MESH
 f32 = jnp.float32
@@ -72,11 +76,10 @@
     pot,
     prior_rot,
     block_rot,
-    filtered_out,
+    fil,
     ritz_out,
     ext0,
     ext1,
-    fil,
     gp,
     gf,
     wp,
@@ -101,6 +104,7 @@
     z_recv,
     out_send,
     out_recv,
+    z_ready,
 ):
     b = lax.axis_index("band")
     d = lax.axis_index("space")
@@ -122,7 +126,10 @@
     barrier = pltpu.get_barrier_semaphore()
     for r in range(1, XS):
         pl.semaphore_signal(barrier, inc=1, device_id=x_peer(r), device_id_type=MESH)
-    pl.semaphore_signal(barrier, inc=1, device_id=z_peer, device_id_type=MESH)
+
+    @pl.when(zh == 0)
+    def _():
+        pl.semaphore_signal(barrier, inc=1, device_id=z_peer, device_id_type=MESH)
 
     @pl.when(has_prev)
     def _():
@@ -137,6 +144,8 @@
             src_ref=src, dst_ref=dst, send_sem=send, recv_sem=recv, device_id=peer, device_id_type=MESH
         )
 
+    parts = [(xp, yh, pl.ds(yh * HALF, HALF)) for xp in range(2) for yh in range(2)]
+
     def chunk(c):
         return pl.ds(c * PER, PER)
 
@@ -145,26 +154,16 @@
         for c in range(CHUNKS)
     ]
     own_prior = [
-        pltpu.make_async_copy(prior.at[:, 0, 2 * x + xp], gp.at[xp, x], local_sem.at[CHUNKS + xp])
-        for xp in range(2)
+        pltpu.make_async_copy(
+            prior.at[:, 0, 2 * x + xp, half], gp.at[xp, x, :, half], local_sem.at[2 * CHUNKS + 2 * xp + yh]
+        )
+        for xp, yh, half in parts
     ]
     own_fil = [
         pltpu.make_async_copy(
-            fil.at[chunk(c), pl.ds(2 * x, 2)], gf.at[x, chunk(c)], local_sem.at[CHUNKS + 2 + c]
-        )
-        for c in range(CHUNKS)
-    ]
-    out_fil = [
-        pltpu.make_async_copy(
-            fil.at[chunk(c)], filtered_out.at[chunk(c), 0], local_sem.at[2 * CHUNKS + 2 + c]
-        )
-        for c in range(CHUNKS)
-    ]
-    own_ritz = [
-        pltpu.make_async_copy(
-            sm.at[xp, x], ritz_out.at[:, 0, 2 * x + xp], local_sem.at[3 * CHUNKS + 2 + xp]
-        )
-        for xp in range(2)
+            fil.at[chunk(c), 0, pl.ds(2 * x, 2)], gf.at[x, chunk(c)], local_sem.at[CHUNKS + c]
+        )
+        for c in range(CHUNKS)
     ]
 
     up0 = [
@@ -214,20 +213,20 @@
     prior_x = [
         [
             remote(
-                prior.at[:, 0, 2 * x_of(r) + xp],
-                gp.at[xp, x],
-                gp_send.at[xp, r - 1],
-                gp_recv.at[xp, r - 1],
+                prior.at[:, 0, 2 * x_of(r) + xp, half],
+                gp.at[xp, x, :, half],
+                gp_send.at[2 * xp + yh, r - 1],
+                gp_recv.at[2 * xp + yh, r - 1],
                 x_peer(r),
             )
             for r in range(1, XS)
         ]
-        for xp in range(2)
+        for xp, yh, half in parts
     ]
     fil_x = [
         [
             remote(
-                fil.at[chunk(c), pl.ds(2 * x_of(r), 2)],
+                fil.at[chunk(c), 0, pl.ds(2 * x_of(r), 2)],
                 gf.at[x, chunk(c)],
                 gf_send.at[c, r - 1],
                 gf_recv.at[c, r - 1],
@@ -238,16 +237,21 @@
         for c in range(CHUNKS)
     ]
 
-    def z_copy(xp, xd):
+    def z_copy(q, r):
+        xp, _, half = parts[q]
+        xd = x_of(r)
         rows = pl.ds((xd * ZH + (1 - zh)) * NB, NB)
-        return remote(pp.at[xp, rows], zr.at[xp, xd], z_send.at[xp, xd], z_recv.at[xp, xd], z_peer)
-
-    def out_copy(xp, r):
         return remote(
-            sm.at[xp, x_of(r)],
-            ritz_out.at[:, 0, 2 * x + xp],
-            out_send.at[xp, r - 1],
-            out_recv.at[xp, r - 1],
+            pp.at[xp, rows, half], zr.at[xp, xd, :, half], z_send.at[q, r], z_recv.at[q, r], z_peer
+        )
+
+    def out_copy(q, r):
+        xp, _, half = parts[q]
+        return remote(
+            sm.at[xp, x_of(r), :, half],
+            ritz_out.at[:, 0, 2 * x + xp, half],
+            out_send.at[q, r - 1],
+            out_recv.at[q, r - 1],
             x_peer(r),
         )
 
@@ -279,7 +283,8 @@
         ext1[:, :, 16:24, :] = jnp.zeros((NB, CX, 8, CZ), f32)
 
     pl.semaphore_wait(
-        barrier, XS + jnp.where(has_prev, 1, 0) + jnp.where(has_next, 1, 0)
+        barrier,
+        XS - 1 + jnp.where(zh == 1, 1, 0) + jnp.where(has_prev, 1, 0) + jnp.where(has_next, 1, 0),
     )
 
     def start_halo(up, down):
@@ -304,6 +309,10 @@
         start_halo(up0[c], down0[c])
     for copy in weights_x + prior_x[0]:
         copy.start()
+
+    @pl.when(zh == 1)
+    def _():
+        pl.semaphore_signal(z_ready, inc=1, device_id=z_peer, device_id_type=MESH)
 
     for c in range(CHUNKS):
         own_block[c].wait()
@@ -326,13 +335,13 @@
             at = c * PER + j
             rows = stencil(ext1, at, band, diagonal)
             for i in range(CX):
-                fil[at, i] = 2.0 * rows[i] - ext0[at, i, 8:16, :]
+                fil[at, 0, i] = 2.0 * rows[i] - ext0[at, i, 8:16, :]
             return carry
 
         lax.fori_loop(0, PER, second, 0)
-        for copy in fil_x[c] + [own_fil[c], out_fil[c]]:
+        for copy in fil_x[c] + [own_fil[c]]:
             copy.start()
-    for copy in prior_x[1]:
+    for copy in prior_x[1] + prior_x[2]:
         copy.start()
 
     wp[x] = prior_rot[...]
@@ -349,13 +358,14 @@
 
     gf_rows = gf.reshape(XS * NB * 2 * CY, CZ)
 
-    def prior_part(xp):
-        own_prior[xp].wait()
-        for copy in prior_x[xp]:
+    def prior_part(q):
+        xp, yh, _ = parts[q]
+        own_prior[q].wait()
+        for copy in prior_x[q]:
             copy.wait_recv()
         gp_rows = gp.at[xp].reshape(XS * NP * CY, CZ)
         pp_rows = pp.at[xp].reshape(NCOL * CY, CZ)
-        for y in range(0, CY, 2):
+        for y in range(yh * HALF, yh * HALF + HALF, 2):
             values = jnp.concatenate(
                 [gp_rows[pl.ds(y + h, XS * NP, stride=CY), :] for h in range(2)], axis=1
             )
@@ -364,9 +374,10 @@
             for h in range(2):
                 pp_rows[pl.ds(y + h, NCOL, stride=CY), :] = total[:, h * CZ : (h + 1) * CZ]
 
-    def block_part(xp):
+    def block_part(q):
+        xp, yh, _ = parts[q]
         pp_rows = pp.at[xp].reshape(NCOL * CY, CZ)
-        for y in range(0, CY, 2):
+        for y in range(yh * HALF, yh * HALF + HALF, 2):
             values = jnp.concatenate(
                 [gf_rows[pl.ds(xp * CY + y + h, XS * NB, stride=2 * CY), :] for h in range(2)], axis=1
             )
@@ -375,38 +386,56 @@
             for h in range(2):
                 at = pl.ds(y + h, NCOL, stride=CY)
                 pp_rows[at, :] = pp_rows[at, :] + total[:, h * CZ : (h + 1) * CZ]
-        for xd in range(XS):
-            z_copy(xp, xd).start()
+
+    def finish(q, r):
+        xp, yh, half = parts[q]
+        xd = x_of(r)
+        low, high = yh * HALF, yh * HALF + HALF
+        z_copy(q, r).wait_recv()
+        columns = pp[xp, pl.ds((xd * ZH + zh) * NB, NB), low:high] + zr[xp, xd, :, low:high]
+        if r == 0:
+            ritz_out[:, 0, 2 * x + xp, low:high] = columns
+        else:
+            sm[xp, xd, :, low:high] = columns
+            out_copy(q, r).start()
 
     prior_part(0)
     for c in range(CHUNKS):
         own_fil[c].wait()
         for copy in fil_x[c]:
             copy.wait_recv()
-    block_part(0)
-    prior_part(1)
-    block_part(1)
-
-    for xp in range(2):
-        for xd in range(XS):
-            z_copy(xp, xd).wait_recv()
-            sm[xp, xd] = pp[xp, pl.ds((xd * ZH + zh) * NB, NB)] + zr[xp, xd]
+
+    @pl.when(zh == 0)
+    def _():
+        pl.semaphore_wait(z_ready, 1)
+
+    steps = [(q, r) for q in range(4) for r in ORDER]
+    for k, (q, r) in enumerate(steps):
+        if k % XS == 0:
+            if q > 0:
+                prior_part(q)
+            block_part(q)
+            if q == 1:
+                for copy in prior_x[3]:
+                    copy.start()
+        if k >= WINDOW:
+            z_copy(*steps[k - WINDOW]).wait_send()
+        z_copy(q, r).start()
+        if k >= LAG:
+            finish(*steps[k - LAG])
+    for k in range(len(steps) - LAG, len(steps)):
+        finish(*steps[k])
+
+    for k in range(len(steps) - WINDOW, len(steps)):
+        z_copy(*steps[k]).wait_send()
+    for q in range(4):
         for r in range(1, XS):
-            out_copy(xp, r).start()
-        own_ritz[xp].start()
-
-    for xp in range(2):
-        own_ritz[xp].wait()
-        for r in range(1, XS):
-            out_copy(xp, r).wait()
-        for xd in range(XS):
-            z_copy(xp, xd).wait_send()
-        for copy in prior_x[xp]:
+            out_copy(q, r).wait()
+        for copy in prior_x[q]:
             copy.wait_send()
     for copy in weights_x:
         copy.wait_send()
     for c in range(CHUNKS):
-        out_fil[c].wait()
         for copy in fil_x[c]:
             copy.wait_send()
 
@@ -429,15 +458,14 @@
     return pl.pallas_call(
         functools.partial(kernel, slabs),
         out_shape=(
-            jax.ShapeDtypeStruct((NB, 1, CX, CY, CZ), f32),
-            jax.ShapeDtypeStruct((NB, 1, CX, CY, CZ), f32),
+            pltpu.VMEM((NB, 1, CX, CY, CZ), f32),
+            pltpu.VMEM((NB, 1, CX, CY, CZ), f32),
         ),
         in_specs=[anywhere, anywhere, whole, whole, whole],
-        out_specs=(anywhere, anywhere),
+        out_specs=(whole, whole),
         scratch_shapes=[
             pltpu.VMEM((NB, CX, 24, CZ), f32),
             pltpu.VMEM((NB, CX, 24, CZ), f32),
-            pltpu.VMEM((NB, CX, CY, CZ), f32),
             pltpu.VMEM((2, XS, NP, CY, CZ), f32),
             pltpu.VMEM((XS, NB, 2, CY, CZ), f32),
             pltpu.VMEM((XS, NP, NCOL), f32),
@@ -449,19 +477,20 @@
             pltpu.VMEM((2, NCOL, CY, CZ), f32),
             pltpu.VMEM((2, XS, NB, CY, CZ), f32),
             pltpu.VMEM((2, XS, NB, CY, CZ), f32),
-            dma((3 * CHUNKS + 4,)),
+            dma((2 * CHUNKS + 4,)),
             dma((4, CHUNKS)),
             dma((4, CHUNKS)),
             dma((XS - 1,)),
             dma((XS - 1,)),
-            dma((2, XS - 1)),
-            dma((2, XS - 1)),
+            dma((4, XS - 1)),
+            dma((4, XS - 1)),
             dma((CHUNKS, XS - 1)),
             dma((CHUNKS, XS - 1)),
-            dma((2, XS)),
-            dma((2, XS)),
-            dma((2, XS - 1)),
-            dma((2, XS - 1)),
+            dma((4, XS)),
+            dma((4, XS)),
+            dma((4, XS - 1)),
+            dma((4, XS - 1)),
+            pltpu.SemaphoreType.REGULAR,
         ],
         compiler_params=pltpu.CompilerParams(
             collective_id=0, has_side_effects=True, vmem_limit_bytes=56 * 1024 * 1024

time: 69 us -> 60.9 us (0.88); the launches traced: 68.7 us -> 59.8 us
  Pallas kernels: 64.3 us -> 57.6 us
  local copies, waits for them, and re-layouts: 3.77 us -> 1.59 us
    pallas_call x1, Pallas kernels: 64.3 us -> 57.6 us  [shards(): pl.pallas_call(functools.partial(kernel, slabs), out_shape=(pltpu.VMEM((N...]
    unnamed x2, local copies, waits for them, and re-layouts: 3.77 us -> 1.59 us
where the time goes in v2:
time: 60.9 us; the launch traced here: 59.8 us
  Pallas kernels  57.6 us (95%)
  local copies, waits for them, and re-layouts  1.59 us (3%)
  between operations  0.64 us (1%)
    pallas_call x1, Pallas kernels, shards(): pl.pallas_call(functools.partial(kernel, slabs), out_shape=(pltpu.VMEM((N...  57.6 us
    unnamed x2, local copies, waits for them, and re-layouts  1.59 us

profile of v2, /device:TPU:56, one launch (start us, length us, event | category | flops | bytes accessed | tf_op | source)
XLA Modules:
  0.0 59.8 jit_solution(4230488163722732907)
XLA Ops:
  0.6 57.6 %filter_and_rotate.1 = (f32[16,1,8,8,128]{4,3,2,1,0:T(8,128)S(1)}, f32[16,1,8,8,128]{4,3,2,1,0:T(8,128)S(1)}) custom-call(f32[48,1,8,8,128]{4,3,2,1,0:T(8,128)} %prior.1, f32[16,1,8,8,128]{4,3,2,1,0:T(8,128)} %block.1, f32[1,8,8,128]{3,2,1,0:T(8,128)} %pot.1, f32[48,128]{1,0:T(8,128)} %prior_rot.1, f32[128,128]{1,0:T(8,128)} %block_rot.1), custom_call_target="tpu_custom_call" | custom-call | flops 402653184 | bytes 4194304 | tf_op jit(solution)/shard_map/filter_and_rotate/pallas_call | solution.py:458
  58.2 0.8 %copy.9 = f32[16,1,8,8,128]{4,3,2,1,0:T(8,128)} copy(f32[16,1,8,8,128]{4,3,2,1,0:T(8,128)S(1)} %get-tuple-element.2) | data formatting | bytes 1048576
  59.0 0.8 %copy.10 = f32[16,1,8,8,128]{4,3,2,1,0:T(8,128)} copy(f32[16,1,8,8,128]{4,3,2,1,0:T(8,128)S(1)} %get-tuple-element.3) | data formatting | bytes 1048576

commit v3 on v2

--- a/solution.py
+++ b/solution.py
@@ -30,7 +30,6 @@
 ZH = 2
 NCOL = 128
 CHUNKS = 4
-WINDOW = 16
 LAG = 8
 HALF = CY // 2
 ORDER = (2, 1, 3, 0)
@@ -409,25 +408,24 @@
     def _():
         pl.semaphore_wait(z_ready, 1)
 
-    steps = [(q, r) for q in range(4) for r in ORDER]
+    steps = [(q, r) for q in range(4) for r in ORDER if q < 2 or r != 0] + [(2, 0), (3, 0)]
+    begins = {steps.index((q, ORDER[0])): q for q in range(4)}
     for k, (q, r) in enumerate(steps):
-        if k % XS == 0:
+        if k in begins:
             if q > 0:
                 prior_part(q)
             block_part(q)
             if q == 1:
                 for copy in prior_x[3]:
                     copy.start()
-        if k >= WINDOW:
-            z_copy(*steps[k - WINDOW]).wait_send()
         z_copy(q, r).start()
         if k >= LAG:
             finish(*steps[k - LAG])
     for k in range(len(steps) - LAG, len(steps)):
         finish(*steps[k])
 
-    for k in range(len(steps) - WINDOW, len(steps)):
-        z_copy(*steps[k]).wait_send()
+    for q, r in steps:
+        z_copy(q, r).wait_send()
     for q in range(4):
         for r in range(1, XS):
             out_copy(q, r).wait()
@@ -450,12 +448,23 @@
             down1[c].wait_send()
 
 
+def write_out(filtered, ritz, filtered_out, ritz_out, sem):
+    copies = [
+        pltpu.make_async_copy(filtered, filtered_out, sem.at[0]),
+        pltpu.make_async_copy(ritz, ritz_out, sem.at[1]),
+    ]
+    for copy in copies:
+        copy.start()
+    for copy in copies:
+        copy.wait()
+
+
 def shards(prior_orbitals, orbital_block, potential, prior_rotation, block_rotation):
     slabs = lax.axis_size("space")
     whole = pl.BlockSpec(memory_space=pltpu.VMEM)
     anywhere = pl.BlockSpec(memory_space=pl.ANY)
     dma = pltpu.SemaphoreType.DMA
-    return pl.pallas_call(
+    kept = pl.pallas_call(
         functools.partial(kernel, slabs),
         out_shape=(
             pltpu.VMEM((NB, 1, CX, CY, CZ), f32),
@@ -500,6 +509,18 @@
         ),
         name="filter_and_rotate",
     )(prior_orbitals, orbital_block, potential, prior_rotation, block_rotation)
+    return pl.pallas_call(
+        write_out,
+        out_shape=(
+            jax.ShapeDtypeStruct((NB, 1, CX, CY, CZ), f32),
+            jax.ShapeDtypeStruct((NB, 1, CX, CY, CZ), f32),
+        ),
+        in_specs=[whole, whole],
+        out_specs=(anywhere, anywhere),
+        scratch_shapes=[dma((2,))],
+        cost_estimate=pl.CostEstimate(flops=0, bytes_accessed=2 * 1024 * 1024, transcendentals=0),
+        name="write_out",
+    )(*[pltpu.with_memory_space_constraint(k, pltpu.VMEM) for k in kept])
 
 
 def solution(mesh):

time: 60.9 us -> 59.3 us (0.974)
  local copies, waits for them, and re-layouts: 1.59 us -> 0 us
    unnamed x2 -> x0, local copies, waits for them, and re-layouts: 1.59 us -> none
    pallas_call x0 -> x1, Pallas kernels: none -> 0.99 us  [shards(): pl.pallas_call(write_out, out_shape=(jax.ShapeDtypeStruct((NB, 1, CX, CY,...]
    pallas_call x1, Pallas kernels: 57.6 us -> 56.9 us  [shards(): pl.pallas_call(functools.partial(kernel, slabs), out_shape=(pltpu.VMEM((N...]
where the time goes in v3:
time: 59.3 us; the launch traced here: 58.5 us
  Pallas kernels  57.9 us (98%)
  between operations  0.64 us (1%)
    pallas_call x1, Pallas kernels, shards(): pl.pallas_call(functools.partial(kernel, slabs), out_shape=(pltpu.VMEM((N...  56.9 us

profile of v3, /device:TPU:56, one launch (start us, length us, event | category | flops | bytes accessed | tf_op | source)
XLA Modules:
  0.0 58.5 jit_solution(4441084385591265386)
XLA Ops:
  0.6 56.9 %filter_and_rotate.1 = (f32[16,1,8,8,128]{4,3,2,1,0:T(8,128)S(1)}, f32[16,1,8,8,128]{4,3,2,1,0:T(8,128)S(1)}) custom-call(f32[48,1,8,8,128]{4,3,2,1,0:T(8,128)} %prior.1, f32[16,1,8,8,128]{4,3,2,1,0:T(8,128)} %block.1, f32[1,8,8,128]{3,2,1,0:T(8,128)} %pot.1, f32[48,128]{1,0:T(8,128)} %prior_rot.1, f32[128,128]{1,0:T(8,128)} %block_rot.1), custom_call_target="tpu_custom_call" | custom-call | flops 402653184 | bytes 4194304 | tf_op jit(solution)/shard_map/filter_and_rotate/pallas_call | solution.py:467
  57.5 1.0 %write_out.1 = (f32[16,1,8,8,128]{4,3,2,1,0:T(8,128)}, f32[16,1,8,8,128]{4,3,2,1,0:T(8,128)}) custom-call(f32[16,1,8,8,128]{4,3,2,1,0:T(8,128)S(1)} %get-tuple-element.4.filtered, f32[16,1,8,8,128]{4,3,2,1,0:T(8,128)S(1)} %get-tuple-element.5.ritz), custom_call_target="tpu_custom_call" | custom-call | bytes 2097152 | tf_op jit(solution)/shard_map/write_out/pallas_call | solution.py:512

commit v4 on v3

--- a/solution.py
+++ b/solution.py
@@ -29,8 +29,8 @@
 XS = 4
 ZH = 2
 NCOL = 128
-CHUNKS = 4
-LAG = 8
+CHUNKS = 8
+LAG = 6
 HALF = CY // 2
 ORDER = (2, 1, 3, 0)
 PER = NB // CHUNKS
@@ -104,6 +104,7 @@
     out_send,
     out_recv,
     z_ready,
+    x_ready,
 ):
     b = lax.axis_index("band")
     d = lax.axis_index("space")
@@ -123,8 +124,12 @@
     next_peer = (b, jnp.minimum(d + 1, slabs - 1))
 
     barrier = pltpu.get_barrier_semaphore()
+
     for r in range(1, XS):
-        pl.semaphore_signal(barrier, inc=1, device_id=x_peer(r), device_id_type=MESH)
+
+        @pl.when(x < x_of(r))
+        def _():
+            pl.semaphore_signal(barrier, inc=1, device_id=x_peer(r), device_id_type=MESH)
 
     @pl.when(zh == 0)
     def _():
@@ -283,7 +288,7 @@
 
     pl.semaphore_wait(
         barrier,
-        XS - 1 + jnp.where(zh == 1, 1, 0) + jnp.where(has_prev, 1, 0) + jnp.where(has_next, 1, 0),
+        x + jnp.where(zh == 1, 1, 0) + jnp.where(has_prev, 1, 0) + jnp.where(has_next, 1, 0),
     )
 
     def start_halo(up, down):
@@ -306,6 +311,16 @@
 
     for c in range(CHUNKS):
         start_halo(up0[c], down0[c])
+    for r in range(1, XS):
+
+        @pl.when(x > x_of(r))
+        def _():
+            pl.semaphore_signal(x_ready, inc=1, device_id=x_peer(r), device_id_type=MESH)
+
+    @pl.when(x < XS - 1)
+    def _():
+        pl.semaphore_wait(x_ready, XS - 1 - x)
+
     for copy in weights_x + prior_x[0]:
         copy.start()
 
@@ -500,6 +515,7 @@
             dma((4, XS - 1)),
             dma((4, XS - 1)),
             pltpu.SemaphoreType.REGULAR,
+            pltpu.SemaphoreType.REGULAR,
         ],
         compiler_params=pltpu.CompilerParams(
             collective_id=0, has_side_effects=True, vmem_limit_bytes=56 * 1024 * 1024

time: 59.3 us -> 58.4 us (0.985)
  the two profiles are of different devices: /device:TPU:56 before, /device:TPU:70 now
where the time goes in v4:
time: 58.4 us; the launch traced here: 58.2 us
  Pallas kernels  57.6 us (99%)
  between operations  0.64 us (1%)
    pallas_call x1, Pallas kernels, shards(): pl.pallas_call(functools.partial(kernel, slabs), out_shape=(pltpu.VMEM((N...  56.6 us

profile of v4, /device:TPU:70, one launch (start us, length us, event | category | flops | bytes accessed | tf_op | source)
XLA Modules:
  0.0 58.2 jit_solution(9570315537643804633)
XLA Ops:
  0.6 56.6 %filter_and_rotate.1 = (f32[16,1,8,8,128]{4,3,2,1,0:T(8,128)S(1)}, f32[16,1,8,8,128]{4,3,2,1,0:T(8,128)S(1)}) custom-call(f32[48,1,8,8,128]{4,3,2,1,0:T(8,128)} %prior.1, f32[16,1,8,8,128]{4,3,2,1,0:T(8,128)} %block.1, f32[1,8,8,128]{3,2,1,0:T(8,128)} %pot.1, f32[48,128]{1,0:T(8,128)} %prior_rot.1, f32[128,128]{1,0:T(8,128)} %block_rot.1), custom_call_target="tpu_custom_call" | custom-call | flops 402653184 | bytes 4194304 | tf_op jit(solution)/shard_map/filter_and_rotate/pallas_call | solution.py:482
  57.2 1.0 %write_out.1 = (f32[16,1,8,8,128]{4,3,2,1,0:T(8,128)}, f32[16,1,8,8,128]{4,3,2,1,0:T(8,128)}) custom-call(f32[16,1,8,8,128]{4,3,2,1,0:T(8,128)S(1)} %get-tuple-element.4.filtered, f32[16,1,8,8,128]{4,3,2,1,0:T(8,128)S(1)} %get-tuple-element.5.ritz), custom_call_target="tpu_custom_call" | custom-call | bytes 2097152 | tf_op jit(solution)/shard_map/write_out/pallas_call | solution.py:528

commit v5 on v4

--- a/solution.py
+++ b/solution.py
@@ -353,7 +353,7 @@
             return carry
 
         lax.fori_loop(0, PER, second, 0)
-        for copy in fil_x[c] + [own_fil[c]]:
+        for copy in (fil_x[c][1], fil_x[c][0], fil_x[c][2], own_fil[c]):
             copy.start()
     for copy in prior_x[1] + prior_x[2]:
         copy.start()

time: 58.4 us -> 58.2 us (level)
  no operation moved by 1% of the time
where the time goes in v5:
time: 58.2 us; the launch traced here: 58.1 us
  Pallas kernels  57.4 us (99%)
  between operations  0.64 us (1%)
    pallas_call x1, Pallas kernels, shards(): pl.pallas_call(functools.partial(kernel, slabs), out_shape=(pltpu.VMEM((N...  56.5 us

profile of v5, /device:TPU:70, one launch (start us, length us, event | category | flops | bytes accessed | tf_op | source)
XLA Modules:
  0.0 58.1 jit_solution(4538129810250595469)
XLA Ops:
  0.6 56.5 %filter_and_rotate.1 = (f32[16,1,8,8,128]{4,3,2,1,0:T(8,128)S(1)}, f32[16,1,8,8,128]{4,3,2,1,0:T(8,128)S(1)}) custom-call(f32[48,1,8,8,128]{4,3,2,1,0:T(8,128)} %prior.1, f32[16,1,8,8,128]{4,3,2,1,0:T(8,128)} %block.1, f32[1,8,8,128]{3,2,1,0:T(8,128)} %pot.1, f32[48,128]{1,0:T(8,128)} %prior_rot.1, f32[128,128]{1,0:T(8,128)} %block_rot.1), custom_call_target="tpu_custom_call" | custom-call | flops 402653184 | bytes 4194304 | tf_op jit(solution)/shard_map/filter_and_rotate/pallas_call | solution.py:482
  57.1 1.0 %write_out.1 = (f32[16,1,8,8,128]{4,3,2,1,0:T(8,128)}, f32[16,1,8,8,128]{4,3,2,1,0:T(8,128)}) custom-call(f32[16,1,8,8,128]{4,3,2,1,0:T(8,128)S(1)} %get-tuple-element.4.filtered, f32[16,1,8,8,128]{4,3,2,1,0:T(8,128)S(1)} %get-tuple-element.5.ritz), custom_call_target="tpu_custom_call" | custom-call | bytes 2097152 | tf_op jit(solution)/shard_map/write_out/pallas_call | solution.py:528
